TPU v7x, 512 devices: a whole 4x8x8 slice. The times are simulated.
512 devices in a mesh: rep: 32 (over x, y), fsdp: 16 (over z, core).
Axes of the slice: x: 4, y: 8, z: 8, core: 2. Of those that a mesh axis runs over, the one named last changes fastest.
Arguments:
- grads: bfloat16 [8, 576, 2048], P(None, 'fsdp')
- momentum: float32 [32, 576, 2048], P('rep', 'fsdp')
- owners: int32 [8], replicated, may hold values from 0 to 31, as said below
Outputs:
- update: bfloat16 [8, 576, 2048], P(None, 'fsdp')
- new_momentum: float32 [32, 576, 2048], P('rep', 'fsdp')
Inputs may be any that keep to these rules, and one draw needn't show every extreme that they name: The owners are distinct; owner 0 and the last replica group always appear.
All inputs are finite; a program needn't handle non-finite values.
Results may differ from a plain program's by a relative error of at most 0.001.
Values may be sent and summed in bfloat16 or wider, within the bound.
No kernel may reach another device: no remote copies, remote signals or barrier semaphores. Data moves between devices by JAX's collectives and lax.ppermute only.
A program may use at most 64 MiB of HBM per device.

v0:
```python
import math
import jax
import jax.numpy as jnp
from jax import lax
from jax.sharding import PartitionSpec as P

ROWS = 576
COLS = 2048
ITERS = 3
EPSILON = 1e-07
MOMENTUM_BETA = 0.95
QUINTIC_A = 3.4445
QUINTIC_B = -4.775
QUINTIC_C = 2.0315


def from_root(shard, axis, root):
    mine = lax.axis_index(axis) == root
    return lax.psum(jnp.where(mine, shard, jnp.zeros_like(shard)), axis)


def matmul(left, right):
    return jnp.dot(left, right, precision=lax.Precision.HIGHEST, preferred_element_type=jnp.float32)


def form_gram(column_block):
    partial_gram = matmul(column_block, column_block.T)
    gram_whole = lax.psum(partial_gram, "fsdp")
    return (gram_whole, gram_whole)


def form_poly(gram_whole):
    return QUINTIC_B * gram_whole + QUINTIC_C * matmul(gram_whole, gram_whole)


def column_orthogonal(steered):
    column_block = lax.all_to_all(steered, "fsdp", split_axis=1, concat_axis=0, tiled=True)
    square_total = lax.psum(jnp.sum(column_block * column_block), "fsdp")
    column_block = column_block / (jnp.sqrt(square_total) + EPSILON)
    for iteration in range(ITERS):
        gram_part, gram_whole = form_gram(column_block)
        polynomial = form_poly(gram_whole)
        column_block = QUINTIC_A * column_block + matmul(polynomial, column_block)
    return lax.all_to_all(column_block, "fsdp", split_axis=0, concat_axis=1, tiled=True)


def shards(grads, momentum, owners):
    factor = 0.2 * math.sqrt(max(ROWS, COLS))
    my_group = lax.axis_index("rep")
    matrix_count = owners.shape[0]
    positions = jnp.arange(matrix_count, dtype=jnp.int32)
    is_mine = owners == my_group
    owns_one = jnp.any(is_mine)
    chosen = jnp.sum(jnp.where(is_mine, positions, 0))
    gradient = lax.dynamic_index_in_dim(grads, chosen, 0, keepdims=False).astype(jnp.float32)
    held_state = momentum[0]
    renewed = jnp.where(owns_one, MOMENTUM_BETA * held_state + gradient, held_state)
    steered = gradient + MOMENTUM_BETA * renewed
    row_block = column_orthogonal(steered)
    scaled_rows = (factor * row_block).astype(jnp.bfloat16)
    delivered = [
        from_root(scaled_rows, "rep", owners[matrix_index]) for matrix_index in range(matrix_count)
    ]
    update = jnp.stack(delivered)
    return (update, renewed[None])


def solution(mesh):
    in_specs = (P(None, "fsdp", None), P("rep", "fsdp", None), P())
    out_specs = (P(None, "fsdp", None), P("rep", "fsdp", None))
    return jax.shard_map(shards, mesh=mesh, in_specs=in_specs, out_specs=out_specs, check_vma=False)
```

profile of v0, /device:TPU:64, one launch (start us, length us, event | category | flops | bytes accessed | tf_op | source)
XLA Modules:
  0.0 647.7 jit_solution(12812694040417416024)
XLA Ops:
  7.2 1.3 fusion.27
  8.5 1.3 compare_reduce_fusion
  11.7 3.2 broadcast_select_fusion
  15.0 1.8 multiply_add_fusion
  16.8 20.5 %all_to_all.23 = f32[36,16,128]{2,0,1:T(8,128)S(1)} all-to-all(f32[36,16,128]{2,0,1:T(8,128)S(1)} %multiply_add_fusion), channel_id=1, replica_groups=mesh['rep'=32,'fsdp'=16] {'fsdp'}, dimensions={1} | all-to-all | bytes 589824 | tf_op jit(solution)/shard_map/all_to_all | solution.py:37
  38.0 23.5 %psum.84 = f32[]{:T(128)} all-reduce(f32[]{:T(128)} %multiply_reduce_fusion), channel_id=1, replica_groups=mesh['rep'=32,'fsdp'=16] {'fsdp'}, use_global_device_ids=true, to_apply=%region_3.4 | all-reduce | flops 1 | bytes 8 | tf_op jit(solution)/shard_map/psum | solution.py:38
  62.3 2.4 fusion.35
  64.8 118.8 %all-reduce.6.cloned.1.call-done = f32[576,576]{1,0:T(8,128)} async-done(((f32[576,576]{1,0:T(8,128)}), f32[576,576]{1,0:T(8,128)}) %all-reduce.6.cloned.1.call-update) | async-done | bytes 1327120 | tf_op jit(solution)/shard_map/psum | solution.py:28
  183.6 6.2 fusion.36
  189.8 1.4 fusion.12
  191.2 2.4 fusion.37
  193.9 117.6 %all-reduce.8.cloned.1.call-done = f32[576,576]{1,0:T(8,128)} async-done(((f32[576,576]{1,0:T(8,128)}), f32[576,576]{1,0:T(8,128)}) %all-reduce.8.cloned.1.call-update) | async-done | bytes 1327120 | tf_op jit(solution)/shard_map/psum | solution.py:28
  311.5 6.2 fusion.38
  317.6 1.4 fusion.15
  319.1 2.4 fusion.39
  321.5 117.8 %all-reduce.10.cloned.1.call-done = f32[576,576]{1,0:T(8,128)} async-done(((f32[576,576]{1,0:T(8,128)}), f32[576,576]{1,0:T(8,128)}) %all-reduce.10.cloned.1.call-update) | async-done | bytes 1327120 | tf_op jit(solution)/shard_map/psum | solution.py:28
  439.3 6.2 fusion.40
  445.5 1.7 fusion.18
  447.9 7.3 %all-to-all-start.1 = ((f32[16,36,128]{2,1,0:T(8,128)}), f32[16,36,128]{2,1,0:T(8,128)S(1)}, u32[]{:S(2)}, u32[]{:S(2)}) async-start(f32[16,36,128]{2,1,0:T(8,128)} %all_to_all.9), calls=%async_computation.1 | async-start | bytes 655360 | tf_op jit(solution)/shard_map/all_to_all | solution.py:44
  460.9 5.0 all-to-all-done.1
  466.8 0.8 stack.33
  468.4 0.8 stack.31
  469.2 0.8 stack.30
  470.7 0.8 stack.28
  471.5 0.8 stack.27
  472.3 162.4 %all-reduce.12.cloned.1.call-done = (bf16[1,36,2048]{2,1,0:T(8,128)(2,1)}, bf16[1,36,2048]{2,1,0:T(8,128)(2,1)}, bf16[1,36,2048]{2,1,0:T(8,128)(2,1)}, bf16[1,36...) async-done(((bf16[1,36,2048]{2,1,0:T(8,128)(2,1)}, ...) | async-done | bytes 1179664 | tf_op jit(solution)/shard_map/psum | solution.py:19
  634.7 1.0 constant_dynamic-update-slice_fusion.7
  635.7 0.9 constant_dynamic-update-slice_fusion.6
  636.6 0.9 constant_dynamic-update-slice_fusion.5
  637.6 0.9 constant_dynamic-update-slice_fusion.4
  638.5 0.9 constant_dynamic-update-slice_fusion.3
  639.5 1.7 copy.29
  (43 shorter events, 5.2 us)
Async XLA Ops:
  7.2 176.4 %all-reduce.6.cloned.1.call-start = ((), (), s32[]{:S(2)}) async-start(), calls=%async_computation.2 | async-start | bytes 2949120 | tf_op jit(solution)/shard_map/psum | solution.py:28
  64.7 246.7 %all-reduce.8.cloned.1.call-start = ((), (), s32[]{:S(2)}) async-start(), calls=%async_computation.3 | async-start | bytes 2949120 | tf_op jit(solution)/shard_map/psum | solution.py:28
  183.6 6.2 copy-start
  193.7 245.6 %all-reduce.10.cloned.1.call-start = ((), (), s32[]{:S(2)}) async-start(), calls=%async_computation.4 | async-start | bytes 2949120 | tf_op jit(solution)/shard_map/psum | solution.py:28
  311.5 6.2 copy-start.1
  439.3 6.2 copy-start.2
  445.5 9.7 %copy-start.6 = (s32[8]{0:T(128)S(1)}, s32[8]{0:T(128)}, u32[]{:S(2)}) copy-start(s32[8]{0:T(128)} %param.5) | copy-start | bytes 100
  447.9 18.0 %all-to-all-start.1 = ((f32[16,36,128]{2,1,0:T(8,128)}), f32[16,36,128]{2,1,0:T(8,128)S(1)}, u32[]{:S(2)}, u32[]{:S(2)}) async-start(f32[16,36,128]{2,1,0:T(8,128)} %all_to_all.9), calls=%async_computation.1 | async-start | bytes 655360 | tf_op jit(solution)/shard_map/all_to_all | solution.py:44
  455.2 179.6 %all-reduce.12.cloned.1.call-start = ((), (), s32[]{:S(2)}) async-start(), calls=%async_computation.5 | async-start | bytes 2621440 | tf_op jit(solution)/shard_map/psum | solution.py:19
  634.7 4.7 copy-start.5
  634.7 4.7 copy-start.4
  634.7 4.8 copy-start.3
Sparse Core Ops, SparseCore 0:
  64.9 118.7 all-reduce.5
  193.8 117.6 all-reduce.7
  321.6 117.6 all-reduce.9
  472.4 162.2 all-reduce.11
where the time goes:
time: 648 us
  waiting for transfers between devices  522 us (81%)
  blocking collectives  44 us (7%)
  matrix products  30.3 us (5%)
  between operations  21.6 us (3%)
  local copies, waits for them, and re-layouts  14.1 us (2%)
  other arithmetic  8.51 us (1%)
  starting transfers between devices  7.61 us (1%)
    psum x3, waiting for transfers between devices, form_gram(): gram_whole = lax.psum(partial_gram, 'fsdp')  354 us
    psum x1, waiting for transfers between devices, from_root(): return lax.psum(jnp.where(mine, shard, jnp.zeros_like(shard)), axis)  162 us
    dot_general x9, matrix products, matmul(): jnp.dot(left, right, precision=lax.Precision.HIGHEST, preferred_element_t...  30.3 us
    psum x1, blocking collectives, column_orthogonal(): square_total = lax.psum(jnp.sum(column_block * column_block), 'fsdp')  23.5 us
    all_to_all x1, blocking collectives, column_orthogonal(): lax.all_to_all(steered, 'fsdp', split_axis=1, concat_axis=0, tiled=True)  20.5 us
  transfers between devices with their start and end apart: 5, of which 5 were waited for; matrix products, arithmetic and copies ran while one was open for 0% of the time, Pallas kernels for 0%

commit v1 on v0

--- a/solution.py
+++ b/solution.py
@@ -25,7 +25,7 @@
 
 def form_gram(column_block):
     partial_gram = matmul(column_block, column_block.T)
-    gram_whole = lax.psum(partial_gram, "fsdp")
+    gram_whole = jnp.sum(lax.all_gather(partial_gram, "fsdp"), axis=0)
     return (gram_whole, gram_whole)
 
 

time: 648 us -> 703 us (1.085)
  waiting for transfers between devices: 522 us -> 556 us
  other arithmetic: 8.51 us -> 35 us
    all_gather x0 -> x3, waiting for transfers between devices: none -> 388 us  [form_gram(): gram_whole = jnp.sum(lax.all_gather(partial_gram, 'fsdp'), axis=0)]
    psum x3 -> x0, waiting for transfers between devices: 354 us -> none  [form_gram(): gram_whole = lax.psum(partial_gram, 'fsdp')]
    reduce_sum x0 -> x3, other arithmetic: none -> 26.5 us  [form_gram(): gram_whole = jnp.sum(lax.all_gather(partial_gram, 'fsdp'), axis=0)]
where the time goes in v1:
time: 703 us; the launch traced here: 702 us
  waiting for transfers between devices  556 us (79%)
  blocking collectives  44 us (6%)
  other arithmetic  35 us (5%)
  matrix products  24.3 us (3%)
  between operations  21.5 us (3%)
  local copies, waits for them, and re-layouts  14.1 us (2%)
  starting transfers between devices  7.28 us (1%)
    all_gather x3, waiting for transfers between devices, form_gram(): gram_whole = jnp.sum(lax.all_gather(partial_gram, 'fsdp'), axis=0)  388 us
    psum x1, waiting for transfers between devices, from_root(): return lax.psum(jnp.where(mine, shard, jnp.zeros_like(shard)), axis)  162 us
    reduce_sum x3, other arithmetic, form_gram(): gram_whole = jnp.sum(lax.all_gather(partial_gram, 'fsdp'), axis=0)  26.5 us
    dot_general x9, matrix products, matmul(): jnp.dot(left, right, precision=lax.Precision.HIGHEST, preferred_element_t...  24.3 us
    psum x1, blocking collectives, column_orthogonal(): square_total = lax.psum(jnp.sum(column_block * column_block), 'fsdp')  23.5 us
    all_to_all x1, blocking collectives, column_orthogonal(): lax.all_to_all(steered, 'fsdp', split_axis=1, concat_axis=0, tiled=True)  20.5 us
  transfers between devices with their start and end apart: 5, of which 5 were waited for; matrix products, arithmetic and copies ran while one was open for 0% of the time, Pallas kernels for 0%

profile of v1, /device:TPU:64, one launch (start us, length us, event | category | flops | bytes accessed | tf_op | source)
XLA Modules:
  0.0 702.2 jit_solution(13333327853101013980)
XLA Ops:
  7.2 1.3 fusion.27
  8.5 1.3 compare_reduce_fusion
  11.7 3.2 broadcast_select_fusion
  15.0 1.8 multiply_add_fusion
  16.8 20.5 %all_to_all.23 = f32[36,16,128]{2,0,1:T(8,128)S(1)} all-to-all(f32[36,16,128]{2,0,1:T(8,128)S(1)} %multiply_add_fusion), channel_id=1, replica_groups=mesh['rep'=32,'fsdp'=16] {'fsdp'}, dimensions={1} | all-to-all | bytes 589824 | tf_op jit(solution)/shard_map/all_to_all | solution.py:37
  38.0 23.5 %psum.63 = f32[]{:T(128)} all-reduce(f32[]{:T(128)} %multiply_reduce_fusion), channel_id=1, replica_groups=mesh['rep'=32,'fsdp'=16] {'fsdp'}, use_global_device_ids=true, to_apply=%region_3.4 | all-reduce | flops 1 | bytes 8 | tf_op jit(solution)/shard_map/psum | solution.py:38
  62.3 2.4 fusion.35
  64.8 130.6 %all-gather.7.cloned.1.call-done = f32[9216,576]{1,0:T(8,128)} async-done(((f32[576,576]{1,0:T(8,128)}), f32[9216,576]{1,0:T(8,128)}) %all-gather.7.cloned.1.call-update) | async-done | bytes 21233680 | tf_op jit(solution)/shard_map/all_gather | solution.py:28
  195.4 8.8 %reduce_sum.47 = f32[576,576]{1,0:T(8,128)S(1)} reduce(f32[16,576,576]{2,1,0:T(8,128)} %bitcast.46, f32[]{:T(128)} %constant.9.clone.1), dimensions={0}, to_apply=%region_4.5 | reduce | flops 4976640 | bytes 22560772 | tf_op jit(solution)/shard_map/reduce_sum | solution.py:28
  204.2 4.2 fusion.36
  208.4 1.5 fusion.12
  209.9 2.4 fusion.37
  212.6 128.8 %all-gather.9.cloned.1.call-done = f32[9216,576]{1,0:T(8,128)} async-done(((f32[576,576]{1,0:T(8,128)}), f32[9216,576]{1,0:T(8,128)}) %all-gather.9.cloned.1.call-update) | async-done | bytes 21233680 | tf_op jit(solution)/shard_map/all_gather | solution.py:28
  341.4 8.8 %reduce_sum.48 = f32[576,576]{1,0:T(8,128)S(1)} reduce(f32[16,576,576]{2,1,0:T(8,128)} %bitcast.47, f32[]{:T(128)} %constant.9.clone.1), dimensions={0}, to_apply=%region_5.6 | reduce | flops 4976640 | bytes 22560772 | tf_op jit(solution)/shard_map/reduce_sum | solution.py:28
  350.1 4.2 fusion.38
  354.3 1.5 fusion.15
  355.8 2.4 fusion.39
  358.2 129.0 %all-gather.11.cloned.1.call-done = f32[9216,576]{1,0:T(8,128)} async-done(((f32[576,576]{1,0:T(8,128)}), f32[9216,576]{1,0:T(8,128)}) %all-gather.11.cloned.1.call-update) | async-done | bytes 21233680 | tf_op jit(solution)/shard_map/all_gather | solution.py:28
  487.3 9.0 %reduce_sum.49 = f32[576,576]{1,0:T(8,128)S(1)} reduce(f32[16,576,576]{2,1,0:T(8,128)} %bitcast.48, f32[]{:T(128)} %constant.9.clone.1), dimensions={0}, to_apply=%region_6.7 | reduce | flops 4976640 | bytes 22560772 | tf_op jit(solution)/shard_map/reduce_sum | solution.py:28
  496.3 4.2 fusion.40
  500.5 1.5 fusion.18
  502.7 6.9 all-to-all-start.1
  515.2 5.1 all-to-all-done.1
  521.3 0.8 stack.28
  525.2 0.8 stack.33
  526.8 162.4 %all-reduce.3.cloned.1.call-done = (bf16[1,36,2048]{2,1,0:T(8,128)(2,1)}, bf16[1,36,2048]{2,1,0:T(8,128)(2,1)}, bf16[1,36,2048]{2,1,0:T(8,128)(2,1)}, bf16[1,36,...) async-done(((bf16[1,36,2048]{2,1,0:T(8,128)(2,1)}, ...) | async-done | bytes 1179664 | tf_op jit(solution)/shard_map/psum | solution.py:19
  689.2 1.0 constant_dynamic-update-slice_fusion.7
  690.2 0.9 constant_dynamic-update-slice_fusion.6
  691.1 0.9 constant_dynamic-update-slice_fusion.5
  692.0 0.9 constant_dynamic-update-slice_fusion.4
  693.0 0.9 constant_dynamic-update-slice_fusion.3
  694.0 1.7 copy.29
  (40 shorter events, 7.4 us)
Async XLA Ops:
  7.2 188.3 %all-gather.7.cloned.1.call-start = ((), (), s32[]{:S(2)}) async-start(), calls=%async_computation.2 | async-start | bytes 25067520 | tf_op jit(solution)/shard_map/all_gather | solution.py:28
  64.8 276.6 %all-gather.9.cloned.1.call-start = ((), (), s32[]{:S(2)}) async-start(), calls=%async_computation.3 | async-start | bytes 25067520 | tf_op jit(solution)/shard_map/all_gather | solution.py:28
  212.3 274.9 %all-gather.11.cloned.1.call-start = ((), (), s32[]{:S(2)}) async-start(), calls=%async_computation.4 | async-start | bytes 25067520 | tf_op jit(solution)/shard_map/all_gather | solution.py:28
  500.4 9.2 %copy-start.3 = (s32[8]{0:T(128)S(1)}, s32[8]{0:T(128)}, u32[]{:S(2)}) copy-start(s32[8]{0:T(128)} %param.5) | copy-start | bytes 100
  502.7 17.7 %all-to-all-start.1 = ((f32[16,36,128]{2,1,0:T(8,128)}), f32[16,36,128]{2,1,0:T(8,128)S(1)}, u32[]{:S(2)}, u32[]{:S(2)}) async-start(f32[16,36,128]{2,1,0:T(8,128)} %all_to_all.9), calls=%async_computation.1 | async-start | bytes 655360 | tf_op jit(solution)/shard_map/all_to_all | solution.py:44
  509.6 179.6 %all-reduce.3.cloned.1.call-start = ((), (), s32[]{:S(2)}) async-start(), calls=%async_computation.5 | async-start | bytes 2621440 | tf_op jit(solution)/shard_map/psum | solution.py:19
  689.2 4.7 copy-start.2
  689.2 4.7 copy-start.1
  689.2 4.8 copy-start
Sparse Core Ops, SparseCore 0:
  64.9 130.5 all-gather.6
  212.5 128.8 all-gather.8
  358.4 128.8 all-gather.10
  526.9 162.2 all-reduce.2
